TPU v7x, 512 devices: a whole 4x8x8 slice. The times are simulated.
512 devices in a mesh: grp: 32 (over z, x), slc: 16 (over y, core).
Axes of the slice: x: 4, y: 8, z: 8, core: 2. Of those that a mesh axis runs over, the one named last changes fastest.
Arguments:
- orbitals: float32 [1024, 48, 2304], P('grp', 'slc'), may hold values from -6 to 6
- local_pot: float32 [1024, 48, 2304], P('grp', 'slc'), may hold values from -1 to 1
- pair_owner: int32 [32, 32, 1], P('grp'), may hold values from 0 to 31; in each aligned block of 32 rows (0 to 31, 32 to 63, ..., all dimensions but the last counted through in order) at most 2 rows name the same one
- pair_remote: int32 [32, 32], P('grp'), may hold values from 0 to 31
- pair_resident: int32 [32, 32], P('grp'), may hold values from 0 to 1
- pair_count: int32 [32, 16], P('grp'), may hold values from 1 to 3, 32 in all within a row
- offsets: int32 [1024, 3], replicated, may hold values from 0 to 23
Outputs:
- applied: float32 [1024, 48, 2304], P('grp', 'slc')
Inputs may be any that keep to these rules, and one draw needn't show every extreme that they name: `pair_owner`: within one group's 32 pairs no owner group is named more than 2 times, and some owner group is named exactly 2 times. `pair_count`: the 16 counts of one group sum to 32, and in every group some device has exactly 3.
All inputs are finite; a program needn't handle non-finite values.
Results may differ from a plain program's by a relative error of at most 0.0003.
Values sent between devices are 32-bit elements; how exact they have to be, the bound alone decides.
A program may use at most 128 MiB of HBM per device.

v0:
```python
import functools

import jax
import jax.numpy as jnp
import numpy as np
from jax import lax
from jax.experimental import pallas as pl
from jax.experimental.pallas import tpu as pltpu
from jax.sharding import PartitionSpec as P

B = 48
CELLS = B * B
LANES = 128
BLOCKS = CELLS // LANES
PLANES = 3
ROWS = 56
GRP = 32
SLC = 16
ORB = 32
PAIRS = 32
HALVES = 2
CHUNKS = ((0, 32), (32, 24))
MARGIN = 9
WIDE = 384
VMEM_LIMIT = 60 * 1024 * 1024

NEAR, OWNER, FAR, SEAT, WANT = 0, 1, 2, 3, 5
GAP, BLOCK, REST = 8, 11, 13


def split_np(values):
    high = values.astype(jnp.bfloat16)
    low = (values - high.astype(np.float64)).astype(jnp.bfloat16)
    return high, low


@functools.cache
def tables():
    k = np.arange(B, dtype=np.float64)
    q = np.sqrt(2.0 / (B + 1)) * np.sin(np.pi * np.outer(k + 1, k + 1) / (B + 1))
    lam = 2.0 - 2.0 * np.cos(np.pi * (k + 1) / (B + 1))
    plane_of = 3 * (np.arange(B) % SLC) + np.arange(B) // SLC
    q_c = np.kron(np.eye(WIDE // B), q)
    q_a = np.zeros((B, LANES))
    q_a[:, :B] = q[plane_of]
    q_high, q_low = split_np(q)
    q_b = np.concatenate([q_high, q_low, q_high], axis=1)
    lam_b = np.broadcast_to(lam[:, None], (B, 2 * LANES)).astype(np.float32)
    lane = np.arange(LANES)
    lam_a = np.where(lane < B, lam[lane % B], 1.0)
    lam_ac = np.zeros((B // 2, 1, 2 * LANES), np.float32)
    for kc in range(B):
        lam_ac[kc // 2, 0, (kc % 2) * LANES : (kc % 2 + 1) * LANES] = lam_a + lam[kc]
    return (*split_np(q_c), *split_np(q_a), q_b, lam_b, lam_ac)


def iota(shape, dim):
    return lax.broadcasted_iota(jnp.int32, shape, dim)


def total_of(mask, values, axis):
    return jnp.sum(jnp.where(mask, values, 0), axis=axis, keepdims=True)


def index_tables(owner, remote, resident, count):
    square = (PAIRS, PAIRS)
    down, across = iota(square, 0), iota(square, 1)

    def as_column(row):
        return total_of(down == across, row, 1)

    owner_col = as_column(owner)
    same = owner_col == owner
    ones = jnp.ones(square, jnp.int32)

    def places(before, axis, other_axis):
        return total_of(same & before, ones, axis), total_of(same, ones, axis)

    rank_row, times_row = places(down < across, 0, 1)
    rank_col, times_col = places(across < down, 1, 0)

    def seats(rank, times, rank_other, times_other, before, axis):
        single, first, second = times == 1, (times == 2) & (rank == 0), rank == 1
        single_o, first_o, second_o = times_other == 1, (times_other == 2) & (rank_other == 0), rank_other == 1
        twice = jnp.sum(jnp.where(second_o, 1, 0), axis=axis, keepdims=True)
        at_first = total_of(before & first_o, ones, axis)
        at_second = total_of(before & second_o, ones, axis)
        filled = twice + total_of(before & single_o, ones, axis)
        late = single & (filled >= SLC)
        half = jnp.where(second | late, 1, 0)
        seat = jnp.where(
            first, at_first, jnp.where(second, at_second, jnp.where(late, filled - SLC + twice, filled))
        )
        return half, seat

    half_row, seat_row = seats(rank_row, times_row, rank_col, times_col, down < across, 0)
    half_col, seat_col = seats(rank_col, times_col, rank_row, times_row, across < down, 1)

    upto = iota((SLC, SLC), 1) <= iota((SLC, SLC), 0)
    running = total_of(upto, count, 1)
    home = jnp.sum(jnp.where(running <= iota((SLC, PAIRS), 1), 1, 0), axis=0, keepdims=True)
    near_col = as_column(home * 2 + resident)
    remote_col = as_column(remote)

    wide = (PAIRS, LANES)
    lane = iota(wide, 1)
    seated = (half_col * SLC + seat_col) == lane
    rows = [jnp.zeros((1, LANES), jnp.int32)] * 8
    rows[NEAR] = total_of(seated, near_col + jnp.zeros(wide, jnp.int32), 0)
    rows[OWNER] = total_of(seated, owner_col + jnp.zeros(wide, jnp.int32), 0)
    rows[FAR] = total_of(seated, owner_col * ORB + remote_col + jnp.zeros(wide, jnp.int32), 0)
    requests = jnp.zeros((GRP, LANES), jnp.int32)
    for h in range(HALVES):
        named = (owner_col == lane) & (half_col == h)
        rows[SEAT + h] = total_of(named, seat_col + jnp.zeros(wide, jnp.int32), 0)
        rows[WANT + h] = ORB + total_of(named, remote_col - ORB + jnp.zeros(wide, jnp.int32), 0)
        asked = (down == owner) & (half_row == h)
        want_col = ORB + total_of(asked, remote - ORB + jnp.zeros(square, jnp.int32), 1)
        requests = jnp.where(iota((GRP, LANES), 1) == h, want_col, requests)
    for n, most in ((NEAR, ORB - 1), (OWNER, GRP - 1), (SEAT, SLC - 1), (SEAT + 1, SLC - 1), (WANT, ORB), (WANT + 1, ORB)):
        rows[n] = jnp.clip(rows[n], 0, most)
    return rows, jnp.clip(requests, 0, ORB)


def shift_rows(rows, offsets, me_g, me_s):
    lane = iota((1, LANES), 1)
    orbital = iota(offsets.shape, 1)
    rows += [jnp.zeros((1, LANES), jnp.int32) for _ in range(8)]
    for h in range(HALVES):
        mine = lane == SLC * h + me_s
        near = me_g * ORB + total_of(mine, rows[NEAR], 1)
        far = total_of(mine, rows[FAR], 1)
        gap = total_of(orbital == near, offsets, 1) - total_of(orbital == far, offsets, 1)
        for k in range(3):
            rows[GAP + k] = jnp.where(lane == h, gap[k : k + 1], rows[GAP + k])
        turn = gap[1:2] * B + gap[2:3]
        for n, sign in enumerate((1, -1)):
            reach = sign * turn + MARGIN * LANES
            reach = jnp.clip(reach, 0, (2 * MARGIN) * LANES - 1)
            block = lax.div(reach, jnp.full_like(reach, LANES))
            rows[BLOCK + n] = jnp.where(lane == h, block, rows[BLOCK + n])
            rows[REST + n] = jnp.where(lane == h, reach - block * LANES, rows[REST + n])


def stack_rows(rows):
    at = iota((len(rows), LANES), 0)
    table = jnp.zeros((len(rows), LANES), jnp.int32)
    for n, row in enumerate(rows):
        table = jnp.where(at == n, row, table)
    return table


def split(values):
    high = values.astype(jnp.bfloat16)
    return high, (values - high.astype(jnp.float32)).astype(jnp.bfloat16)


def dot(left, right, dims=((1,), (0,))):
    return lax.dot_general(left, right, (dims, ((), ())), preferred_element_type=jnp.float32)


def plane_at(shape, dim):
    row = iota(shape, dim)
    return 3 * lax.rem(row, SLC) + lax.div(row, SLC)


GROUPS = [slice(g * WIDE, (g + 1) * WIDE) for g in range(CELLS // WIDE)]


def wire_places():
    for q in range(BLOCKS):
        for p in range(PLANES):
            yield (
                pl.ds(3 * q + p, SLC, stride=ROWS),
                slice(p * SLC, (p + 1) * SLC),
                slice(q * LANES, (q + 1) * LANES),
            )


def lane_shift(blocks, block, rest):
    loaded = [blocks[block + q] for q in range(BLOCKS + 1)]
    near, over = jnp.concatenate(loaded[:-1], axis=0), jnp.concatenate(loaded[1:], axis=0)
    high, low = split(jnp.concatenate([near, over], axis=1))
    square = (2 * LANES, LANES)
    onehot = jnp.where(iota(square, 0) == iota(square, 1) + rest, 1.0, 0.0).astype(jnp.bfloat16)
    out = dot(high, onehot) + dot(low, onehot)
    return jnp.concatenate([out[q * B : (q + 1) * B] for q in range(BLOCKS)], axis=1)


def pair_fields(gap, there, back, near_box, far_box, near_field, far_field, consts, scratch):
    qc_high, qc_low, qa_high, qa_low, q_b, lam_b, lam_ac = consts
    psi, moved, blocks, modes = scratch
    e0, e1, e2 = gap
    lane = iota((8, CELLS), 1)[:1]
    at_b, at_c = lax.div(lane, B) + e1, lax.rem(lane, B) + e2
    inside = (at_b >= 0) & (at_b < B) & (at_c >= 0) & (at_c < B)
    inside = jnp.where(inside, 1.0, 0.0).astype(jnp.float32)
    onehot = jnp.where(plane_at((B, B), 0) + e0 == plane_at((B, B), 1), 1.0, 0.0).astype(jnp.bfloat16)
    for where, rows, cols in wire_places():
        psi[rows, cols] = near_box[where, :]
        blocks[MARGIN + cols.start // LANES, rows, :] = far_box[where, :]
    high, low = split(lane_shift(blocks, *there) * inside)
    moved[...] = dot(onehot, high) + dot(onehot, low)

    density = jnp.concatenate([psi[:, cols] * moved[:, cols] for cols in GROUPS], axis=0)
    high, low = split(density)
    part = dot(high, qc_high[...]) + dot(low, qc_high[...]) + dot(high, qc_low[...])
    for g, cols in enumerate(GROUPS):
        high, low = split(part[g * B : (g + 1) * B])
        over = ((0,), (0,))
        modes[cols, :] = (
            dot(high, qa_high[...], over) + dot(low, qa_high[...], over) + dot(high, qa_low[...], over)
        )

    def along_b(values):
        high, low = split(values)
        return dot(q_b[...], jnp.concatenate([high, high, low], axis=0))

    def weigh(i, _):
        even, odd = pl.ds(2 * i, B, stride=B), pl.ds(2 * i + 1, B, stride=B)
        values = along_b(jnp.concatenate([modes[even, :], modes[odd, :]], axis=1))
        values = along_b(values / (lam_b[...] + lam_ac[i]))
        modes[even, :] = values[:, :LANES]
        modes[odd, :] = values[:, LANES:]
        return 0

    lax.fori_loop(0, B // 2, weigh, 0, unroll=2)

    parts = []
    for cols in GROUPS:
        high, low = split(modes[cols, :])
        over = ((1,), (1,))
        parts.append(
            dot(qa_high[...], high, over) + dot(qa_high[...], low, over) + dot(qa_low[...], high, over)
        )
    high, low = split(jnp.concatenate(parts, axis=0))
    potential = dot(high, qc_high[...]) + dot(low, qc_high[...]) + dot(high, qc_low[...])
    for g, cols in enumerate(GROUPS):
        here = potential[g * B : (g + 1) * B]
        moved[:, cols] = here * moved[:, cols]
        high, low = split(here * psi[:, cols] * inside[:, cols])
        over = ((0,), (0,))
        apart = dot(onehot, high, over) + dot(onehot, low, over)
        for n in range(WIDE // LANES):
            blocks[MARGIN + cols.start // LANES + n] = apart[:, n * LANES : (n + 1) * LANES]
    far = lane_shift(blocks, *back)
    for where, rows, cols in wire_places():
        near_field[where, :] = moved[rows, cols]
        far_field[where, :] = far[rows, cols]


def peer(me, i, count):
    return lax.rem(me + (i // 2 + 1) * (1 - 2 * (i % 2)) + count, count)


def part_of(slot, count):
    return pl.ds(pl.multiple_of(slot * count, 8), count)


def rows_of(slot, row, count):
    return pl.ds(pl.multiple_of(slot * ROWS + row, 8), count)


N = len(CHUNKS)


def exchange_kernel(*refs):
    names = iter(refs)

    def take(count=1):
        out = [next(names) for _ in range(count)]
        return out[0] if count == 1 else out

    def halves():
        return take(HALVES)

    def chunked():
        return [take(N) for _ in range(HALVES)]

    owner, remote, resident, count_row, offsets, orb_hbm = take(6)
    consts_hbm = take(7)
    near_back, answers = halves(), halves()
    table_out, req_recv = take(2)
    orb, slabs, want, table_smem, req_smem = take(5)
    consts = take(7)
    near_send, near_box, far_box, near_field, far_field = (halves() for _ in range(5))
    g_send, g_recv, f_send, f_back, a_send = (chunked() for _ in range(5))
    scratch = take(4)
    local_sem, const_sem, rq_s, rq_r, near_s, near_r, nback_s, nback_r = take(8)
    grp_s, grp_r, far_s, far_r, fback_s, fback_r, ans_s, ans_r = take(8)

    me_g, me_s = lax.axis_index("grp"), lax.axis_index("slc")

    def each(axis, action):
        me, count = (me_g, GRP) if axis == "grp" else (me_s, SLC)

        def step(i, _):
            action(peer(me, i, count))
            return 0

        lax.fori_loop(0, count - 1, step, 0)

    orb_copy = pltpu.make_async_copy(orb_hbm, orb, local_sem.at[2])
    orb_copy.start()
    const_copies = [pltpu.make_async_copy(a, b, const_sem.at[n]) for n, (a, b) in enumerate(zip(consts_hbm, consts))]
    for copy in const_copies:
        copy.start()
    barrier = pltpu.get_barrier_semaphore()
    each("grp", lambda there: pl.semaphore_signal(barrier, inc=1, device_id={"grp": there}))
    each("slc", lambda there: pl.semaphore_signal(barrier, inc=1, device_id={"slc": there}))

    rows, requests = index_tables(owner[...], remote[...], resident[...], count_row[...])
    shift_rows(rows, offsets[...], me_g, me_s)
    table_out[...] = stack_rows(rows)
    want[...] = requests.reshape(GRP, 1, LANES)
    local = pltpu.make_async_copy(table_out, table_smem, local_sem.at[0])
    local.start()
    orb_copy.wait()
    for q in range(BLOCKS):
        for p in range(PLANES):
            slabs[:ORB, 3 * q + p, :] = orb[p, :, q * LANES : (q + 1) * LANES]
    slabs[:ORB, 54:56, :] = jnp.zeros((ORB, 2, LANES), jnp.float32)
    slabs[ORB] = jnp.zeros((ROWS, LANES), jnp.float32)
    blocks = scratch[2]
    blocks[...] = jnp.zeros_like(blocks)
    local.wait()
    pl.semaphore_wait(barrier, GRP + SLC - 2)

    def remote_copy(src, dst, send, recv, axis, there):
        return pltpu.make_async_remote_copy(
            src_ref=src, dst_ref=dst, send_sem=send, recv_sem=recv, device_id={axis: there}
        )

    def req_copy(there, slot):
        return remote_copy(want.at[there], req_recv.at[slot], rq_s.at[0], rq_r.at[0], "grp", there)

    def near_copy(h, there, slot):
        return remote_copy(
            near_send[h].at[part_of(there, ROWS)], near_box[h].at[part_of(slot, ROWS)],
            near_s.at[h], near_r.at[h], "slc", there,
        )

    def grp_copy(h, c, there, slot):
        return remote_copy(
            g_send[h][c].at[there], g_recv[h][c].at[slot], grp_s.at[N * h + c], grp_r.at[N * h + c], "grp", there
        )

    def far_copy(h, c, there, slot):
        row, count = CHUNKS[c]
        return remote_copy(
            f_send[h][c].at[there], far_box[h].at[rows_of(slot, row, count)],
            far_s.at[N * h + c], far_r.at[N * h + c], "slc", there,
        )

    def fback_copy(h, c, there, slot):
        row, count = CHUNKS[c]
        return remote_copy(
            far_field[h].at[rows_of(there, row, count)], f_back[h][c].at[slot],
            fback_s.at[N * h + c], fback_r.at[N * h + c], "slc", there,
        )

    def nback_copy(h, there, slot):
        return remote_copy(
            near_field[h].at[part_of(there, ROWS)], near_back[h].at[part_of(slot, ROWS)],
            nback_s.at[h], nback_r.at[h], "slc", there,
        )

    def ans_copy(h, c, there, slot):
        row, count = CHUNKS[c]
        return remote_copy(
            a_send[h][c].at[there], answers[h].at[rows_of(slot, row, count)],
            ans_s.at[N * h + c], ans_r.at[N * h + c], "grp", there,
        )

    def all_of(ref, size, send, recv, axis):
        me, count = (me_g, GRP) if axis == "grp" else (me_s, SLC)
        whole = ref.at[pl.ds(0, size)]
        return remote_copy(whole, whole, send, recv, axis, peer(me, 0, count))

    def all_req():
        return all_of(req_recv, GRP - 1, rq_s.at[0], rq_r.at[0], "grp")

    def all_near(h):
        return all_of(near_box[h], (SLC - 1) * ROWS, near_s.at[h], near_r.at[h], "slc")

    def all_grp(h, c):
        return all_of(g_recv[h][c], GRP - 1, grp_s.at[N * h + c], grp_r.at[N * h + c], "grp")

    def all_far(h, c):
        return all_of(f_send[h][c], SLC - 1, far_s.at[N * h + c], far_r.at[N * h + c], "slc")

    def all_fback(h, c):
        return all_of(f_back[h][c], SLC - 1, fback_s.at[N * h + c], fback_r.at[N * h + c], "slc")

    def all_nback(h):
        return all_of(near_back[h], (SLC - 1) * ROWS, nback_s.at[h], nback_r.at[h], "slc")

    def all_ans(h, c):
        return all_of(a_send[h][c], GRP - 1, ans_s.at[N * h + c], ans_r.at[N * h + c], "grp")

    def send_near(h):
        def one(there):
            near_send[h][part_of(there, ROWS), :] = slabs[table_smem[NEAR, SLC * h + there]]
            near_copy(h, there, me_s).start()

        each("slc", one)
        near_box[h][part_of(me_s, ROWS), :] = slabs[table_smem[NEAR, SLC * h + me_s]]

    def send_grp(h, c):
        row, count = CHUNKS[c]

        def one(there):
            g_send[h][c][there] = slabs[req_smem[there, 0, h], row : row + count, :]
            grp_copy(h, c, there, me_g).start()

        each("grp", one)
        g_recv[h][c][me_g] = slabs[table_smem[WANT + h, me_g], row : row + count, :]

    def forward_far(h, c):
        row, count = CHUNKS[c]
        all_grp(h, c).wait_recv()

        def one(there):
            f_send[h][c][there] = g_recv[h][c][table_smem[OWNER, SLC * h + there]]
            far_copy(h, c, there, me_s).start()

        each("slc", one)
        far_box[h][rows_of(me_s, row, count), :] = g_recv[h][c][table_smem[OWNER, SLC * h + me_s]]

    def compute(h):
        all_near(h).wait_recv()
        for c in range(N):
            all_far(h, c).wait_recv()
        gap = [table_smem[GAP + k, h] for k in range(3)]
        there, back = [(table_smem[BLOCK + n, h], table_smem[REST + n, h]) for n in range(2)]
        pair_fields(gap, there, back, near_box[h], far_box[h], near_field[h], far_field[h], consts, scratch)

    def send_fields(h):
        for c, (row, count) in enumerate(CHUNKS):
            each("slc", lambda there: fback_copy(h, c, there, me_s).start())
            f_back[h][c][me_s] = far_field[h][rows_of(me_s, row, count), :]

    def send_near_fields(h):
        each("slc", lambda there: nback_copy(h, there, me_s).start())
        near_back[h][part_of(me_s, ROWS), :] = near_field[h][part_of(me_s, ROWS), :]

    def send_answers(h, c):
        row, count = CHUNKS[c]
        all_fback(h, c).wait_recv()

        def one(there):
            a_send[h][c][there] = f_back[h][c][table_smem[SEAT + h, there]]
            ans_copy(h, c, there, me_g).start()

        each("grp", one)
        answers[h][rows_of(me_g, row, count), :] = f_back[h][c][table_smem[SEAT + h, me_g]]

    each("grp", lambda there: req_copy(there, me_g).start())
    req_recv[me_g] = want[me_g]
    send_near(0)
    all_req().wait_recv()
    asked = pltpu.make_async_copy(req_recv, req_smem, local_sem.at[1])
    asked.start()
    asked.wait()
    for c in range(N):
        send_grp(0, c)
    for c in range(N):
        forward_far(0, c)
        send_grp(1, c)
    send_near(1)
    for copy in const_copies:
        copy.wait()
    compute(0)
    send_fields(0)
    for c in range(N):
        forward_far(1, c)
        send_answers(0, c)
    send_near_fields(0)
    compute(1)
    send_fields(1)
    for c in range(N):
        send_answers(1, c)
    send_near_fields(1)

    all_req().wait_send()
    for h in range(HALVES):
        all_near(h).wait_send()
        all_nback(h).wait()
        for c in range(N):
            all_grp(h, c).wait_send()
            all_far(h, c).wait_send()
            all_fback(h, c).wait_send()
            all_ans(h, c).wait()


def exchange(owner, remote, resident, count, offsets, orb):
    vmem = pl.BlockSpec(memory_space=pltpu.VMEM)

    def slots(number):
        return pltpu.VMEM((number * ROWS, LANES), jnp.float32)

    def out(number):
        return jax.ShapeDtypeStruct((number * ROWS, LANES), jnp.float32)

    def chunked(number):
        return [pltpu.VMEM((number, rows, LANES), jnp.float32) for _ in range(HALVES) for _, rows in CHUNKS]

    hbm = pl.BlockSpec(memory_space=pltpu.HBM)
    consts = [jnp.asarray(t) for t in tables()]

    def sems(number):
        return [pltpu.SemaphoreType.DMA((number,))] * 2

    return pl.pallas_call(
        exchange_kernel,
        out_shape=[
            *[out(SLC)] * HALVES,
            *[out(GRP)] * HALVES,
            jax.ShapeDtypeStruct((16, LANES), jnp.int32),
            jax.ShapeDtypeStruct((GRP, 1, LANES), jnp.int32),
        ],
        in_specs=[vmem, vmem, vmem, vmem, vmem, hbm, *[hbm] * len(consts)],
        out_specs=[vmem] * 6,
        scratch_shapes=[
            pltpu.VMEM(orb.shape, jnp.float32),
            pltpu.VMEM((ORB + 1, ROWS, LANES), jnp.float32),
            pltpu.VMEM((GRP, 1, LANES), jnp.int32),
            pltpu.SMEM((16, LANES), jnp.int32),
            pltpu.SMEM((GRP, 1, LANES), jnp.int32),
            *[pltpu.VMEM(t.shape, t.dtype) for t in consts],
            *[slots(SLC)] * (5 * HALVES),
            *chunked(GRP),
            *chunked(GRP),
            *chunked(SLC),
            *chunked(SLC),
            *chunked(GRP),
            *[pltpu.VMEM((B, CELLS), jnp.float32)] * 2,
            pltpu.VMEM((2 * MARGIN + BLOCKS, B, LANES), jnp.float32),
            pltpu.VMEM((CELLS, LANES), jnp.float32),
            pltpu.SemaphoreType.DMA((3,)),
            pltpu.SemaphoreType.DMA((len(consts),)),
            *sems(1),
            *sems(HALVES),
            *sems(HALVES),
            *sems(HALVES * N),
            *sems(HALVES * N),
            *sems(HALVES * N),
            *sems(HALVES * N),
        ],
        compiler_params=pltpu.CompilerParams(
            collective_id=0, has_side_effects=True, vmem_limit_bytes=VMEM_LIMIT
        ),
        name="exchange",
    )(owner, remote, resident, count, offsets, orb, *consts)


def sum_kernel(table, requested, orb_hbm, pot_hbm, near_0, near_1, answers_0, answers_1, out, total, orb, pot, sem):
    copies = [
        pltpu.make_async_copy(orb_hbm, orb, sem.at[0]),
        pltpu.make_async_copy(pot_hbm, pot, sem.at[1]),
    ]
    for copy in copies:
        copy.start()
    total[...] = jnp.zeros_like(total)

    def add(source, t, place):
        total[part_of(place, ROWS), :] += source[part_of(t, ROWS), :]

    def add_near(t, _):
        add(near_0, t, table[NEAR, t])
        add(near_1, t, table[NEAR, SLC + t])
        return 0

    def add_far(t, _):
        add(answers_0, t, requested[t, 0, 0])
        add(answers_1, t, requested[t, 0, 1])
        return 0

    lax.fori_loop(0, SLC, add_near, 0)
    lax.fori_loop(0, GRP, add_far, 0)
    for copy in copies:
        copy.wait()
    for q in range(BLOCKS):
        for p in range(PLANES):
            cols = slice(q * LANES, (q + 1) * LANES)
            field = total[pl.ds(3 * q + p, ORB, stride=ROWS), :]
            out[p, :, cols] = pot[p, :, cols] * orb[p, :, cols] - field


def sums(table, requested, orb, pot, fields):
    smem, vmem = pl.BlockSpec(memory_space=pltpu.SMEM), pl.BlockSpec(memory_space=pltpu.VMEM)
    return pl.pallas_call(
        sum_kernel,
        out_shape=jax.ShapeDtypeStruct(orb.shape, jnp.float32),
        in_specs=[smem, smem, *[pl.BlockSpec(memory_space=pltpu.HBM)] * 2, *[vmem] * 4],
        out_specs=vmem,
        scratch_shapes=[
            pltpu.VMEM(((ORB + 1) * ROWS, LANES), jnp.float32),
            *[pltpu.VMEM(orb.shape, jnp.float32)] * 2,
            pltpu.SemaphoreType.DMA((2,)),
        ],
        compiler_params=pltpu.CompilerParams(vmem_limit_bytes=VMEM_LIMIT),
        name="sums",
    )(table, requested, orb, pot, *fields)


def per_device(orbitals, local_pot, pair_owner, pair_remote, pair_resident, pair_count, offsets):
    orb, pot = jnp.transpose(orbitals, (1, 0, 2)), jnp.transpose(local_pot, (1, 0, 2))
    *fields, table, requested = exchange(
        pair_owner.reshape(1, PAIRS), pair_remote, pair_resident, pair_count, offsets.T, orb
    )
    return jnp.transpose(sums(table, requested, orb, pot, fields), (1, 0, 2))


def solution(mesh):
    in_specs = (
        P("grp", "slc", None),
        P("grp", "slc", None),
        P("grp", None, None),
        P("grp", None),
        P("grp", None),
        P("grp", None),
        P(),
    )
    return jax.shard_map(
        per_device, mesh=mesh, in_specs=in_specs, out_specs=P("grp", "slc", None), check_vma=False
    )
```

profile of v0, /device:TPU:1, one launch (start us, length us, event | category | flops | bytes accessed | tf_op | source)
XLA Modules:
  0.0 136.5 jit_solution(3881891601261606322)
XLA Ops:
  0.0 132.2 %exchange.1 = (f32[896,128]{1,0:T(8,128)}, f32[896,128]{1,0:T(8,128)}, f32[1792,128]{1,0:T(8,128)}, f32[1792,128]{1,0:T(8,128)}, s32[16,128]{1,0:T(8,128)}, /*index=5*/s32[32,1,128]{2,1,0:T(1,128)}) custom-call(s32[1,32]{1,0:T(1,128)} %bitcast.9, s32[1,32]{1,0:T(1,128)} %refs_1_.1, s32[1,32]{1,0:T(1,128)} %refs_2_.1, s32[1,16]{1,0:T(1,128)} %refs_3_.1, ...), custom_call_target="tpu_custom_call" | custom-call | tf_op jit(solution)/shard_map/exchange/pallas_call | solution.py:514
  132.2 4.3 %sums.1 = f32[3,32,2304]{2,1,0:T(8,128)} custom-call(s32[16,128]{1,0:T(8,128)} %get-tuple-element.11.table, s32[32,1,128]{2,1,0:T(1,128)} %get-tuple-element.12.requested, f32[3,32,2304]{2,1,0:T(8,128)} %bitcast.6, f32[3,32,2304]{2,1,0:T(8,128)} %bitcast.7, f32[896,128]{1,0:T(8,128)} %get-tuple-element.13.near_0, f32[896,128]{1,0:T(8,128)} %get-tuple-element.14.near_1, ...), custom_call_target="tpu_custom_call" | custom-call | tf_op jit(solution)/shard_map/sums/pallas_call | solution.py:592
where the time goes:
time: 137 us
  Pallas kernels  137 us (100%)
    pallas_call x1, Pallas kernels, exchange(): pl.pallas_call(exchange_kernel, out_shape=[*[out(SLC)] * HALVES, *[out(GR...  132 us
    pallas_call x1, Pallas kernels, sums(): pl.pallas_call(sum_kernel, out_shape=jax.ShapeDtypeStruct(orb.shape, jnp....  4.35 us

commit v1 on v0

--- a/solution.py
+++ b/solution.py
@@ -19,7 +19,8 @@
 ORB = 32
 PAIRS = 32
 HALVES = 2
-CHUNKS = ((0, 32), (32, 24))
+CHUNKS = ((0, 40), (40, 16))
+BACK_CHUNKS = ((0, 16), (16, 40))
 MARGIN = 9
 WIDE = 384
 VMEM_LIMIT = 60 * 1024 * 1024
@@ -353,7 +354,7 @@
         )
 
     def fback_copy(h, c, there, slot):
-        row, count = CHUNKS[c]
+        row, count = BACK_CHUNKS[c]
         return remote_copy(
             far_field[h].at[rows_of(there, row, count)], f_back[h][c].at[slot],
             fback_s.at[N * h + c], fback_r.at[N * h + c], "slc", there,
@@ -366,7 +367,7 @@
         )
 
     def ans_copy(h, c, there, slot):
-        row, count = CHUNKS[c]
+        row, count = BACK_CHUNKS[c]
         return remote_copy(
             a_send[h][c].at[there], answers[h].at[rows_of(slot, row, count)],
             ans_s.at[N * h + c], ans_r.at[N * h + c], "grp", there,
@@ -427,16 +428,20 @@
         each("slc", one)
         far_box[h][rows_of(me_s, row, count), :] = g_recv[h][c][table_smem[OWNER, SLC * h + me_s]]
 
-    def compute(h):
+    def await_boxes(h):
         all_near(h).wait_recv()
         for c in range(N):
             all_far(h, c).wait_recv()
+
+    def compute(h):
         gap = [table_smem[GAP + k, h] for k in range(3)]
         there, back = [(table_smem[BLOCK + n, h], table_smem[REST + n, h]) for n in range(2)]
         pair_fields(gap, there, back, near_box[h], far_box[h], near_field[h], far_field[h], consts, scratch)
 
     def send_fields(h):
-        for c, (row, count) in enumerate(CHUNKS):
+        for c, (row, count) in enumerate(BACK_CHUNKS):
+            if c:
+                all_fback(h, c - 1).wait_send()
             each("slc", lambda there: fback_copy(h, c, there, me_s).start())
             f_back[h][c][me_s] = far_field[h][rows_of(me_s, row, count), :]
 
@@ -445,7 +450,7 @@
         near_back[h][part_of(me_s, ROWS), :] = near_field[h][part_of(me_s, ROWS), :]
 
     def send_answers(h, c):
-        row, count = CHUNKS[c]
+        row, count = BACK_CHUNKS[c]
         all_fback(h, c).wait_recv()
 
         def one(there):
@@ -462,19 +467,23 @@
     asked = pltpu.make_async_copy(req_recv, req_smem, local_sem.at[1])
     asked.start()
     asked.wait()
-    for c in range(N):
-        send_grp(0, c)
-    for c in range(N):
-        forward_far(0, c)
-        send_grp(1, c)
+    send_grp(0, 0)
     send_near(1)
+    all_grp(0, 0).wait_send()
+    send_grp(0, 1)
+    forward_far(0, 0)
+    send_grp(1, 0)
+    forward_far(0, 1)
     for copy in const_copies:
         copy.wait()
+    await_boxes(0)
+    send_grp(1, 1)
     compute(0)
     send_fields(0)
     for c in range(N):
         forward_far(1, c)
         send_answers(0, c)
+    await_boxes(1)
     send_near_fields(0)
     compute(1)
     send_fields(1)
@@ -486,10 +495,11 @@
     for h in range(HALVES):
         all_near(h).wait_send()
         all_nback(h).wait()
+        all_fback(h, N - 1).wait_send()
         for c in range(N):
-            all_grp(h, c).wait_send()
+            if (h, c) != (0, 0):
+                all_grp(h, c).wait_send()
             all_far(h, c).wait_send()
-            all_fback(h, c).wait_send()
             all_ans(h, c).wait()
 
 
@@ -502,8 +512,8 @@
     def out(number):
         return jax.ShapeDtypeStruct((number * ROWS, LANES), jnp.float32)
 
-    def chunked(number):
-        return [pltpu.VMEM((number, rows, LANES), jnp.float32) for _ in range(HALVES) for _, rows in CHUNKS]
+    def chunked(number, chunks):
+        return [pltpu.VMEM((number, rows, LANES), jnp.float32) for _ in range(HALVES) for _, rows in chunks]
 
     hbm = pl.BlockSpec(memory_space=pltpu.HBM)
     consts = [jnp.asarray(t) for t in tables()]
@@ -529,11 +539,11 @@
             pltpu.SMEM((GRP, 1, LANES), jnp.int32),
             *[pltpu.VMEM(t.shape, t.dtype) for t in consts],
             *[slots(SLC)] * (5 * HALVES),
-            *chunked(GRP),
-            *chunked(GRP),
-            *chunked(SLC),
-            *chunked(SLC),
-            *chunked(GRP),
+            *chunked(GRP, CHUNKS),
+            *chunked(GRP, CHUNKS),
+            *chunked(SLC, CHUNKS),
+            *chunked(SLC, BACK_CHUNKS),
+            *chunked(GRP, BACK_CHUNKS),
             *[pltpu.VMEM((B, CELLS), jnp.float32)] * 2,
             pltpu.VMEM((2 * MARGIN + BLOCKS, B, LANES), jnp.float32),
             pltpu.VMEM((CELLS, LANES), jnp.float32),

time: 137 us -> 136 us (level)
  Pallas kernels: 137 us -> 134 us
    pallas_call x1, Pallas kernels: 132 us -> 130 us  [exchange(): pl.pallas_call(exchange_kernel, out_shape=[*[out(SLC)] * HALVES, *[out(GR...]
where the time goes in v1:
time: 136 us; the launch traced here: 134 us
  Pallas kernels  134 us (99%)
    pallas_call x1, Pallas kernels, exchange(): pl.pallas_call(exchange_kernel, out_shape=[*[out(SLC)] * HALVES, *[out(GR...  130 us
    pallas_call x1, Pallas kernels, sums(): pl.pallas_call(sum_kernel, out_shape=jax.ShapeDtypeStruct(orb.shape, jnp....  4.35 us

profile of v1, /device:TPU:1, one launch (start us, length us, event | category | flops | bytes accessed | tf_op | source)
XLA Modules:
  0.0 134.4 jit_solution(16069981442555771730)
XLA Ops:
  0.0 130.0 %exchange.1 = (f32[896,128]{1,0:T(8,128)}, f32[896,128]{1,0:T(8,128)}, f32[1792,128]{1,0:T(8,128)}, f32[1792,128]{1,0:T(8,128)}, s32[16,128]{1,0:T(8,128)}, /*index=5*/s32[32,1,128]{2,1,0:T(1,128)}) custom-call(s32[1,32]{1,0:T(1,128)} %bitcast.9, s32[1,32]{1,0:T(1,128)} %refs_1_.1, s32[1,32]{1,0:T(1,128)} %refs_2_.1, s32[1,16]{1,0:T(1,128)} %refs_3_.1, ...), custom_call_target="tpu_custom_call" | custom-call | tf_op jit(solution)/shard_map/exchange/pallas_call | solution.py:524
  130.1 4.3 %sums.1 = f32[3,32,2304]{2,1,0:T(8,128)} custom-call(s32[16,128]{1,0:T(8,128)} %get-tuple-element.11.table, s32[32,1,128]{2,1,0:T(1,128)} %get-tuple-element.12.requested, f32[3,32,2304]{2,1,0:T(8,128)} %bitcast.6, f32[3,32,2304]{2,1,0:T(8,128)} %bitcast.7, f32[896,128]{1,0:T(8,128)} %get-tuple-element.13.near_0, f32[896,128]{1,0:T(8,128)} %get-tuple-element.14.near_1, ...), custom_call_target="tpu_custom_call" | custom-call | tf_op jit(solution)/shard_map/sums/pallas_call | solution.py:602

commit v2 on v1

--- a/solution.py
+++ b/solution.py
@@ -23,6 +23,8 @@
 BACK_CHUNKS = ((0, 16), (16, 40))
 MARGIN = 9
 WIDE = 384
+PART = 256
+HELD = WIDE // 2
 VMEM_LIMIT = 60 * 1024 * 1024
 
 NEAR, OWNER, FAR, SEAT, WANT = 0, 1, 2, 3, 5
@@ -41,17 +43,20 @@
     q = np.sqrt(2.0 / (B + 1)) * np.sin(np.pi * np.outer(k + 1, k + 1) / (B + 1))
     lam = 2.0 - 2.0 * np.cos(np.pi * (k + 1) / (B + 1))
     plane_of = 3 * (np.arange(B) % SLC) + np.arange(B) // SLC
-    q_c = np.kron(np.eye(WIDE // B), q)
-    q_a = np.zeros((B, LANES))
-    q_a[:, :B] = q[plane_of]
+    q_c = np.zeros((WIDE, 2 * PART))
+    for b in range(WIDE // B):
+        for c in range(B):
+            q_c[b * B : (b + 1) * B, PART * (c % 2) + b * (B // 2) + c // 2] = q[:, c]
+    q_a = np.zeros((2 * B, LANES))
+    q_a[:B, :B] = q[plane_of]
+    q_a[B:, LANES // 2 : LANES // 2 + B] = q[plane_of]
     q_high, q_low = split_np(q)
     q_b = np.concatenate([q_high, q_low, q_high], axis=1)
     lam_b = np.broadcast_to(lam[:, None], (B, 2 * LANES)).astype(np.float32)
-    lane = np.arange(LANES)
-    lam_a = np.where(lane < B, lam[lane % B], 1.0)
-    lam_ac = np.zeros((B // 2, 1, 2 * LANES), np.float32)
+    lam_ac = np.ones((B // 4, 1, 2 * LANES), np.float32)
     for kc in range(B):
-        lam_ac[kc // 2, 0, (kc % 2) * LANES : (kc % 2 + 1) * LANES] = lam_a + lam[kc]
+        start = (kc // 2 % 2) * LANES + (kc % 2) * (LANES // 2)
+        lam_ac[kc // 4, 0, start : start + B] = lam + lam[kc]
     return (*split_np(q_c), *split_np(q_a), q_b, lam_b, lam_ac)
 
 
@@ -206,36 +211,35 @@
     density = jnp.concatenate([psi[:, cols] * moved[:, cols] for cols in GROUPS], axis=0)
     high, low = split(density)
     part = dot(high, qc_high[...]) + dot(low, qc_high[...]) + dot(high, qc_low[...])
-    for g, cols in enumerate(GROUPS):
-        high, low = split(part[g * B : (g + 1) * B])
+    for g in range(len(GROUPS)):
+        mine = part[g * B : (g + 1) * B]
+        high, low = split(jnp.concatenate([mine[:, :PART], mine[:, PART:]], axis=0))
         over = ((0,), (0,))
-        modes[cols, :] = (
-            dot(high, qa_high[...], over) + dot(low, qa_high[...], over) + dot(high, qa_low[...], over)
-        )
+        out = dot(high, qa_high[...], over) + dot(low, qa_high[...], over) + dot(high, qa_low[...], over)
+        modes[g * HELD : (g + 1) * HELD, :] = out[:HELD]
 
     def along_b(values):
         high, low = split(values)
         return dot(q_b[...], jnp.concatenate([high, high, low], axis=0))
 
     def weigh(i, _):
-        even, odd = pl.ds(2 * i, B, stride=B), pl.ds(2 * i + 1, B, stride=B)
-        values = along_b(jnp.concatenate([modes[even, :], modes[odd, :]], axis=1))
+        left, right = pl.ds(2 * i, B, stride=B // 2), pl.ds(2 * i + 1, B, stride=B // 2)
+        values = along_b(jnp.concatenate([modes[left, :], modes[right, :]], axis=1))
         values = along_b(values / (lam_b[...] + lam_ac[i]))
-        modes[even, :] = values[:, :LANES]
-        modes[odd, :] = values[:, LANES:]
+        modes[left, :] = values[:, :LANES]
+        modes[right, :] = values[:, LANES:]
         return 0
 
-    lax.fori_loop(0, B // 2, weigh, 0, unroll=2)
+    lax.fori_loop(0, B // 4, weigh, 0, unroll=4)
 
     parts = []
-    for cols in GROUPS:
-        high, low = split(modes[cols, :])
-        over = ((1,), (1,))
-        parts.append(
-            dot(qa_high[...], high, over) + dot(qa_high[...], low, over) + dot(qa_low[...], high, over)
-        )
+    over = ((1,), (1,))
+    for g in range(len(GROUPS)):
+        high, low = split(modes[g * HELD : g * HELD + PART, :])
+        out = dot(qa_high[...], high, over) + dot(qa_high[...], low, over) + dot(qa_low[...], high, over)
+        parts.append(jnp.concatenate([out[:B], out[B:]], axis=1))
     high, low = split(jnp.concatenate(parts, axis=0))
-    potential = dot(high, qc_high[...]) + dot(low, qc_high[...]) + dot(high, qc_low[...])
+    potential = dot(high, qc_high[...], over) + dot(low, qc_high[...], over) + dot(high, qc_low[...], over)
     for g, cols in enumerate(GROUPS):
         here = potential[g * B : (g + 1) * B]
         moved[:, cols] = here * moved[:, cols]
@@ -324,6 +328,7 @@
     slabs[ORB] = jnp.zeros((ROWS, LANES), jnp.float32)
     blocks = scratch[2]
     blocks[...] = jnp.zeros_like(blocks)
+    scratch[3][CELLS // 2 :, :] = jnp.zeros((PART - HELD, LANES), jnp.float32)
     local.wait()
     pl.semaphore_wait(barrier, GRP + SLC - 2)
 
@@ -428,20 +433,16 @@
         each("slc", one)
         far_box[h][rows_of(me_s, row, count), :] = g_recv[h][c][table_smem[OWNER, SLC * h + me_s]]
 
-    def await_boxes(h):
+    def compute(h):
         all_near(h).wait_recv()
         for c in range(N):
             all_far(h, c).wait_recv()
-
-    def compute(h):
         gap = [table_smem[GAP + k, h] for k in range(3)]
         there, back = [(table_smem[BLOCK + n, h], table_smem[REST + n, h]) for n in range(2)]
         pair_fields(gap, there, back, near_box[h], far_box[h], near_field[h], far_field[h], consts, scratch)
 
     def send_fields(h):
         for c, (row, count) in enumerate(BACK_CHUNKS):
-            if c:
-                all_fback(h, c - 1).wait_send()
             each("slc", lambda there: fback_copy(h, c, there, me_s).start())
             f_back[h][c][me_s] = far_field[h][rows_of(me_s, row, count), :]
 
@@ -467,23 +468,19 @@
     asked = pltpu.make_async_copy(req_recv, req_smem, local_sem.at[1])
     asked.start()
     asked.wait()
-    send_grp(0, 0)
+    for c in range(N):
+        send_grp(0, c)
     send_near(1)
-    all_grp(0, 0).wait_send()
-    send_grp(0, 1)
-    forward_far(0, 0)
-    send_grp(1, 0)
-    forward_far(0, 1)
+    for c in range(N):
+        forward_far(0, c)
+        send_grp(1, c)
     for copy in const_copies:
         copy.wait()
-    await_boxes(0)
-    send_grp(1, 1)
     compute(0)
     send_fields(0)
     for c in range(N):
         forward_far(1, c)
         send_answers(0, c)
-    await_boxes(1)
     send_near_fields(0)
     compute(1)
     send_fields(1)
@@ -495,11 +492,10 @@
     for h in range(HALVES):
         all_near(h).wait_send()
         all_nback(h).wait()
-        all_fback(h, N - 1).wait_send()
         for c in range(N):
-            if (h, c) != (0, 0):
-                all_grp(h, c).wait_send()
+            all_grp(h, c).wait_send()
             all_far(h, c).wait_send()
+            all_fback(h, c).wait_send()
             all_ans(h, c).wait()
 
 
@@ -546,7 +542,7 @@
             *chunked(GRP, BACK_CHUNKS),
             *[pltpu.VMEM((B, CELLS), jnp.float32)] * 2,
             pltpu.VMEM((2 * MARGIN + BLOCKS, B, LANES), jnp.float32),
-            pltpu.VMEM((CELLS, LANES), jnp.float32),
+            pltpu.VMEM((CELLS // 2 + PART - HELD, LANES), jnp.float32),
             pltpu.SemaphoreType.DMA((3,)),
             pltpu.SemaphoreType.DMA((len(consts),)),
             *sems(1),
@@ -564,31 +560,30 @@
     )(owner, remote, resident, count, offsets, orb, *consts)
 
 
-def sum_kernel(table, requested, orb_hbm, pot_hbm, near_0, near_1, answers_0, answers_1, out, total, orb, pot, sem):
-    copies = [
-        pltpu.make_async_copy(orb_hbm, orb, sem.at[0]),
-        pltpu.make_async_copy(pot_hbm, pot, sem.at[1]),
-    ]
+def sum_kernel(table, requested, *refs):
+    hbm, out, total, held, sem = refs[:6], refs[6], refs[7], refs[8:14], refs[14]
+    copies = [pltpu.make_async_copy(a, b, sem.at[n]) for n, (a, b) in enumerate(zip(hbm, held))]
     for copy in copies:
         copy.start()
+    near, answers, (orb, pot) = held[:2], held[2:4], held[4:]
     total[...] = jnp.zeros_like(total)
-
-    def add(source, t, place):
-        total[part_of(place, ROWS), :] += source[part_of(t, ROWS), :]
-
-    def add_near(t, _):
-        add(near_0, t, table[NEAR, t])
-        add(near_1, t, table[NEAR, SLC + t])
-        return 0
-
-    def add_far(t, _):
-        add(answers_0, t, requested[t, 0, 0])
-        add(answers_1, t, requested[t, 0, 1])
-        return 0
-
-    lax.fori_loop(0, SLC, add_near, 0)
-    lax.fori_loop(0, GRP, add_far, 0)
-    for copy in copies:
+    for h in range(HALVES):
+        copies[h].wait()
+
+        def add_near(t, _, h=h):
+            total[part_of(table[NEAR, SLC * h + t], ROWS), :] += near[h][part_of(t, ROWS), :]
+            return 0
+
+        lax.fori_loop(0, SLC, add_near, 0, unroll=2)
+    for h in range(HALVES):
+        copies[HALVES + h].wait()
+
+        def add_far(t, _, h=h):
+            total[part_of(requested[t, 0, h], ROWS), :] += answers[h][part_of(t, ROWS), :]
+            return 0
+
+        lax.fori_loop(0, GRP, add_far, 0, unroll=2)
+    for copy in copies[2 * HALVES :]:
         copy.wait()
     for q in range(BLOCKS):
         for p in range(PLANES):
@@ -598,20 +593,21 @@
 
 
 def sums(table, requested, orb, pot, fields):
-    smem, vmem = pl.BlockSpec(memory_space=pltpu.SMEM), pl.BlockSpec(memory_space=pltpu.VMEM)
+    smem, vmem, hbm = (pl.BlockSpec(memory_space=m) for m in (pltpu.SMEM, pltpu.VMEM, pltpu.HBM))
+    inputs = [*fields, orb, pot]
     return pl.pallas_call(
         sum_kernel,
         out_shape=jax.ShapeDtypeStruct(orb.shape, jnp.float32),
-        in_specs=[smem, smem, *[pl.BlockSpec(memory_space=pltpu.HBM)] * 2, *[vmem] * 4],
+        in_specs=[smem, smem, *[hbm] * len(inputs)],
         out_specs=vmem,
         scratch_shapes=[
             pltpu.VMEM(((ORB + 1) * ROWS, LANES), jnp.float32),
-            *[pltpu.VMEM(orb.shape, jnp.float32)] * 2,
-            pltpu.SemaphoreType.DMA((2,)),
+            *[pltpu.VMEM(x.shape, jnp.float32) for x in inputs],
+            pltpu.SemaphoreType.DMA((len(inputs),)),
         ],
         compiler_params=pltpu.CompilerParams(vmem_limit_bytes=VMEM_LIMIT),
         name="sums",
-    )(table, requested, orb, pot, *fields)
+    )(table, requested, *inputs)
 
 
 def per_device(orbitals, local_pot, pair_owner, pair_remote, pair_resident, pair_count, offsets):

time: 136 us -> 126 us (0.926)
  Pallas kernels: 134 us -> 125 us
    pallas_call x1, Pallas kernels: 130 us -> 121 us  [exchange(): pl.pallas_call(exchange_kernel, out_shape=[*[out(SLC)] * HALVES, *[out(GR...]
where the time goes in v2:
time: 126 us; the launch traced here: 125 us
  Pallas kernels  125 us (99%)
    pallas_call x1, Pallas kernels, exchange(): pl.pallas_call(exchange_kernel, out_shape=[*[out(SLC)] * HALVES, *[out(GR...  121 us
    pallas_call x1, Pallas kernels, sums(): pl.pallas_call(sum_kernel, out_shape=jax.ShapeDtypeStruct(orb.shape, jnp....  4.53 us

profile of v2, /device:TPU:1, one launch (start us, length us, event | category | flops | bytes accessed | tf_op | source)
XLA Modules:
  0.0 125.3 jit_solution(1956231727336614770)
XLA Ops:
  0.0 120.7 %exchange.1 = (f32[896,128]{1,0:T(8,128)}, f32[896,128]{1,0:T(8,128)}, f32[1792,128]{1,0:T(8,128)}, f32[1792,128]{1,0:T(8,128)}, s32[16,128]{1,0:T(8,128)}, /*index=5*/s32[32,1,128]{2,1,0:T(1,128)}) custom-call(s32[1,32]{1,0:T(1,128)} %bitcast.9, s32[1,32]{1,0:T(1,128)} %refs_1_.1, s32[1,32]{1,0:T(1,128)} %refs_2_.1, s32[1,16]{1,0:T(1,128)} %refs_3_.1, ...), custom_call_target="tpu_custom_call" | custom-call | tf_op jit(solution)/shard_map/exchange/pallas_call | solution.py:520
  120.7 4.5 %sums.1 = f32[3,32,2304]{2,1,0:T(8,128)} custom-call(s32[16,128]{1,0:T(8,128)} %get-tuple-element.11.table, s32[32,1,128]{2,1,0:T(1,128)} %get-tuple-element.12.requested, f32[896,128]{1,0:T(8,128)} %get-tuple-element.13.refs_0_, f32[896,128]{1,0:T(8,128)} %get-tuple-element.14.refs_1_, f32[1792,128]{1,0:T(8,128)} %get-tuple-element.15.refs_2_, ...), custom_call_target="tpu_custom_call" | custom-call | tf_op jit(solution)/shard_map/sums/pallas_call | solution.py:598

commit v3 on v2

--- a/solution.py
+++ b/solution.py
@@ -19,8 +19,8 @@
 ORB = 32
 PAIRS = 32
 HALVES = 2
-CHUNKS = ((0, 40), (40, 16))
-BACK_CHUNKS = ((0, 16), (16, 40))
+CHUNKS = ((0, 40), (40, 14))
+BACK_CHUNKS = ((0, 16), (16, 38))
 MARGIN = 9
 WIDE = 384
 PART = 256
@@ -230,7 +230,7 @@
         modes[right, :] = values[:, LANES:]
         return 0
 
-    lax.fori_loop(0, B // 4, weigh, 0, unroll=4)
+    lax.fori_loop(0, B // 4, weigh, 0, unroll=6)
 
     parts = []
     over = ((1,), (1,))
@@ -291,7 +291,7 @@
     near_send, near_box, far_box, near_field, far_field = (halves() for _ in range(5))
     g_send, g_recv, f_send, f_back, a_send = (chunked() for _ in range(5))
     scratch = take(4)
-    local_sem, const_sem, rq_s, rq_r, near_s, near_r, nback_s, nback_r = take(8)
+    local_sem, const_sem, own_sem, rq_s, rq_r, near_s, near_r, nback_s, nback_r = take(9)
     grp_s, grp_r, far_s, far_r, fback_s, fback_r, ans_s, ans_r = take(8)
 
     me_g, me_s = lax.axis_index("grp"), lax.axis_index("slc")
@@ -303,7 +303,7 @@
             action(peer(me, i, count))
             return 0
 
-        lax.fori_loop(0, count - 1, step, 0)
+        lax.fori_loop(0, count - 1, step, 0, unroll=5 if axis == "slc" else 1)
 
     orb_copy = pltpu.make_async_copy(orb_hbm, orb, local_sem.at[2])
     orb_copy.start()
@@ -378,6 +378,15 @@
             ans_s.at[N * h + c], ans_r.at[N * h + c], "grp", there,
         )
 
+    def own_near(h):
+        mine = part_of(me_s, ROWS)
+        return pltpu.make_async_copy(near_field[h].at[mine], near_back[h].at[mine], own_sem.at[h])
+
+    def own_answer(h, c):
+        row, count = BACK_CHUNKS[c]
+        there = answers[h].at[rows_of(me_g, row, count)]
+        return pltpu.make_async_copy(a_send[h][c].at[me_g], there, own_sem.at[HALVES + N * h + c])
+
     def all_of(ref, size, send, recv, axis):
         me, count = (me_g, GRP) if axis == "grp" else (me_s, SLC)
         whole = ref.at[pl.ds(0, size)]
@@ -448,7 +457,7 @@
 
     def send_near_fields(h):
         each("slc", lambda there: nback_copy(h, there, me_s).start())
-        near_back[h][part_of(me_s, ROWS), :] = near_field[h][part_of(me_s, ROWS), :]
+        own_near(h).start()
 
     def send_answers(h, c):
         row, count = BACK_CHUNKS[c]
@@ -459,7 +468,8 @@
             ans_copy(h, c, there, me_g).start()
 
         each("grp", one)
-        answers[h][rows_of(me_g, row, count), :] = f_back[h][c][table_smem[SEAT + h, me_g]]
+        a_send[h][c][me_g] = f_back[h][c][table_smem[SEAT + h, me_g]]
+        own_answer(h, c).start()
 
     each("grp", lambda there: req_copy(there, me_g).start())
     req_recv[me_g] = want[me_g]
@@ -492,11 +502,13 @@
     for h in range(HALVES):
         all_near(h).wait_send()
         all_nback(h).wait()
+        own_near(h).wait()
         for c in range(N):
             all_grp(h, c).wait_send()
             all_far(h, c).wait_send()
             all_fback(h, c).wait_send()
             all_ans(h, c).wait()
+            own_answer(h, c).wait()
 
 
 def exchange(owner, remote, resident, count, offsets, orb):
@@ -526,7 +538,7 @@
             jax.ShapeDtypeStruct((GRP, 1, LANES), jnp.int32),
         ],
         in_specs=[vmem, vmem, vmem, vmem, vmem, hbm, *[hbm] * len(consts)],
-        out_specs=[vmem] * 6,
+        out_specs=[*[hbm] * (2 * HALVES), vmem, vmem],
         scratch_shapes=[
             pltpu.VMEM(orb.shape, jnp.float32),
             pltpu.VMEM((ORB + 1, ROWS, LANES), jnp.float32),
@@ -545,6 +557,7 @@
             pltpu.VMEM((CELLS // 2 + PART - HELD, LANES), jnp.float32),
             pltpu.SemaphoreType.DMA((3,)),
             pltpu.SemaphoreType.DMA((len(consts),)),
+            pltpu.SemaphoreType.DMA((HALVES + HALVES * N,)),
             *sems(1),
             *sems(HALVES),
             *sems(HALVES),

time: 126 us -> 124 us (0.984)
    pallas_call x1, Pallas kernels: 121 us -> 119 us  [exchange(): pl.pallas_call(exchange_kernel, out_shape=[*[out(SLC)] * HALVES, *[out(GR...]
where the time goes in v3:
time: 124 us
  Pallas kernels  124 us (100%)
    pallas_call x1, Pallas kernels, exchange(): pl.pallas_call(exchange_kernel, out_shape=[*[out(SLC)] * HALVES, *[out(GR...  119 us
    pallas_call x1, Pallas kernels, sums(): pl.pallas_call(sum_kernel, out_shape=jax.ShapeDtypeStruct(orb.shape, jnp....  4.53 us

profile of v3, /device:TPU:1, one launch (start us, length us, event | category | flops | bytes accessed | tf_op | source)
XLA Modules:
  0.0 123.9 jit_solution(9648317511276156636)
XLA Ops:
  0.0 119.4 %exchange.1 = (f32[896,128]{1,0:T(8,128)}, f32[896,128]{1,0:T(8,128)}, f32[1792,128]{1,0:T(8,128)}, f32[1792,128]{1,0:T(8,128)}, s32[16,128]{1,0:T(8,128)}, /*index=5*/s32[32,1,128]{2,1,0:T(1,128)}) custom-call(s32[1,32]{1,0:T(1,128)} %bitcast.9, s32[1,32]{1,0:T(1,128)} %refs_1_.1, s32[1,32]{1,0:T(1,128)} %refs_2_.1, s32[1,16]{1,0:T(1,128)} %refs_3_.1, ...), custom_call_target="tpu_custom_call" | custom-call | tf_op jit(solution)/shard_map/exchange/pallas_call | solution.py:532
  119.4 4.5 %sums.1 = f32[3,32,2304]{2,1,0:T(8,128)} custom-call(s32[16,128]{1,0:T(8,128)} %get-tuple-element.11.table, s32[32,1,128]{2,1,0:T(1,128)} %get-tuple-element.12.requested, f32[896,128]{1,0:T(8,128)} %get-tuple-element.13.refs_0_, f32[896,128]{1,0:T(8,128)} %get-tuple-element.14.refs_1_, f32[1792,128]{1,0:T(8,128)} %get-tuple-element.15.refs_2_, ...), custom_call_target="tpu_custom_call" | custom-call | tf_op jit(solution)/shard_map/sums/pallas_call | solution.py:611
